TPU v7x, 512 devices: a whole 4x8x8 slice. The times are simulated.
512 devices in a mesh: tm: 128 (over x_hi, z, y), lat: 4 (over x_lo, core).
Axes of the slice: x: 4 (x_hi: 2, x_lo: 2; x = x_hi * 2 + x_lo), y: 8, z: 8, core: 2. Of those that a mesh axis runs over, the one named last changes fastest.
Arguments:
- increments: float32 [128, 4, 32, 384], P('tm', None, 'lat'), may hold values from -6 to 6
- correlation: float32 [128, 4, 32, 384], P('tm', None, 'lat'), may hold values from 0.3 to 1, as said below
- coefficients: float32 [6, 32, 384], P(None, 'lat'), may hold values from -0.15 to 0.2, as said below
- obs_cell: int32 [128, 4096], P('tm', 'lat'), may hold values from 0 to 49151
- obs_value: float32 [128, 4096], P('tm', 'lat'), may hold values from -6 to 6
- obs_weight: float32 [128, 4096], P('tm', 'lat'), may hold values from 0.5 to 4
- obs_count: int32 [128, 4], P('tm', 'lat'), may hold values from 512 to 1024, as said below
- obs_step: int32 [128], P('tm'), may hold values from 1 to 4
Outputs:
- gradient: float32 [128, 4, 32, 384], P('tm', None, 'lat')
- direction: float32 [128, 4, 32, 384], P('tm', None, 'lat')
Inputs may be any that keep to these rules, and one draw needn't show every extreme that they name: `correlation`: per cell rates of several magnitudes, varying between subwindows. Positive wave coefficients and diffusivities, drifts of either sign. `obs_count`: in every subwindow some slab has all 1024 slots live.
All inputs are finite; a program needn't handle non-finite values.
Results may differ from a plain program's by a relative error of at most 0.0003.
Values sent between devices are 32-bit elements; how exact they have to be, the bound alone decides.
No kernel may reach another device: no remote copies, remote signals or barrier semaphores. Data moves between devices by JAX's collectives and lax.ppermute only.
A program may use at most 128 MiB of HBM per device.

v0:
```python
import jax
import jax.numpy as jnp
from jax import lax
from jax.experimental import pallas as pl
from jax.experimental.pallas import tpu as pltpu
from jax.sharding import PartitionSpec as P

STEPS = 4
FIELDS = 4
NY = 32
LON = 384
ROWS = 8
SLABS = 4
WIN = 3 * ROWS
MID = 16
LANE = 128
TILES = LON // LANE
PACK = 11 * ROWS
KINDS = 4
TIMES = 128
CHUNK = 256


def lon_roll(field, by):
    return pltpu.roll(field, by % LON, 1)


def row_roll(field, by):
    return pltpu.roll(field, by % WIN, 0)


def step(state, coef, sign):
    h, u, v, q = state
    keep, kx, kw, ky, ks, cx, cw, cy, cs = coef["common"]
    qe, qw, qn, qs = coef["forward" if sign > 0 else "backward"]

    def sides(f):
        return lon_roll(f, -1), lon_roll(f, 1), row_roll(f, -1), row_roll(f, 1)

    def spread(f, e, w, n, s):
        return keep * f + (kx * e + kw * w) + (ky * n + ks * s)

    he, hw, hn, hs = sides(h)
    ue, uw, un, us = sides(u)
    ve, vw, vn, vs = sides(v)
    te, tw, tn, ts = sides(q)
    div = (cw * uw - cx * u) + (cs * vs - cy * v)
    gx = cx * (he - h)
    gy = cy * (hn - h)
    new_h = spread(h, he, hw, hn, hs)
    new_u = spread(u, ue, uw, un, us)
    new_v = spread(v, ve, vw, vn, vs)
    new_q = keep * q + (qe * te + qw * tw) + (qn * tn + qs * ts)
    if sign > 0:
        return new_h + div, new_u - gx, new_v - gy, new_q
    return new_h - div, new_u + gx, new_v + gy, new_q


def split(value):
    big = value.astype(jnp.bfloat16)
    return big, (value - big.astype(jnp.float32)).astype(jnp.bfloat16)


def subwindow_kernel(obs_step, packed, rates, out, buf):
    slab = lax.axis_index("lat")
    obs_at = obs_step[0]

    def window(base):
        parts = []
        for offset in (-1, 0, 1):
            at = slab + offset
            inside = jnp.logical_and(at >= 0, at < SLABS)
            first = jnp.clip(at, 0, SLABS - 1) * PACK + base
            part = packed[pl.ds(pl.multiple_of(first, ROWS), ROWS), :]
            parts.append(jnp.where(inside, part, 0.0))
        return jnp.concatenate(parts, axis=0)

    row = lax.broadcasted_iota(jnp.int32, (WIN, LON), 0) + (slab - 1) * ROWS
    in_grid = jnp.logical_and(row >= 0, row < NY)
    inc = tuple(window(f * ROWS) for f in range(FIELDS))
    cx, cy, ax, by, kx, ky = (window((FIELDS + i) * ROWS) for i in range(6))

    def south(c):
        return jnp.where(in_grid, row_roll(c, 1), 0.0)

    kw, ks, cw, cs = lon_roll(kx, 1), south(ky), lon_roll(cx, 1), south(cy)
    aw, bs = lon_roll(ax, 1), south(by)
    keep = 1.0 - ((kx + kw) + (ky + ks))
    coef = {
        "common": (keep, kx, kw, ky, ks, cx, cw, cy, cs),
        "forward": (kx - ax, kw + aw, ky - by, ks + bs),
        "backward": (kx + ax, kw - aw, ky + by, ks - bs),
    }
    state = inc
    seen = inc
    for turn in range(STEPS):
        state = step(state, coef, 1.0)
        if turn == 0:
            seen = state
        else:
            seen = tuple(jnp.where(obs_at == turn + 1, a, b) for a, b in zip(state, seen, strict=True))
    end = state

    for f in range(FIELDS):
        buf[f * WIN : (f + 1) * WIN, :] = seen[f]
    edge = (WIN - MID) // 2
    table = jnp.concatenate(
        [
            buf[f * WIN + edge : f * WIN + edge + MID, t * LANE : (t + 1) * LANE]
            for t in range(TILES)
            for f in range(FIELDS)
        ],
        axis=0,
    )
    high = table.shape[0]
    table_parts = jnp.concatenate(split(table), axis=1)

    hi_iota = lax.broadcasted_iota(jnp.int32, (high, LANE), 0)
    lo_iota = lax.broadcasted_iota(jnp.int32, (LANE, LANE), 0)
    forcing = jnp.zeros((high, 2 * LANE), jnp.float32)
    for owner in range(SLABS):
        base = owner * PACK + 10 * ROWS
        cell = packed[base : base + ROWS, 0:LANE].astype(jnp.int32)
        value = packed[base : base + ROWS, LANE : 2 * LANE]
        weight = packed[base : base + ROWS, 2 * LANE : 3 * LANE]
        low = jnp.bitwise_and(cell, LANE - 1)
        tile_row = jnp.right_shift(cell, 7)
        field_row = jnp.right_shift(tile_row * 21846, 16)
        tile = tile_row - field_row * TILES
        field = jnp.right_shift(field_row, 5)
        rel = jnp.bitwise_and(field_row, NY - 1) - (slab * ROWS - edge)
        near = jnp.logical_and(rel >= 0, rel < MID)
        spot = jnp.where(near, tile * (FIELDS * MID) + field * MID + rel, -1)
        for pair in range(ROWS // 2):
            rows = (2 * pair, 2 * pair + 1)
            pick = jnp.concatenate(
                [jnp.where(hi_iota == spot[r : r + 1, :], 1.0, 0.0) for r in rows], axis=1
            ).astype(jnp.bfloat16)
            match = jnp.concatenate([lo_iota == low[r : r + 1, :] for r in rows], axis=1)
            columns = lax.dot_general(
                table_parts, pick, (((0,), (0,)), ((), ())), preferred_element_type=jnp.float32
            )
            columns = columns[:LANE] + columns[LANE:]
            sampled = jnp.sum(jnp.where(match, columns, 0.0), axis=0, keepdims=True)
            wide_value = jnp.concatenate([value[r : r + 1, :] for r in rows], axis=1)
            wide_weight = jnp.concatenate([weight[r : r + 1, :] for r in rows], axis=1)
            depart = wide_weight * (sampled - wide_value)
            rounded = depart.astype(jnp.bfloat16).astype(jnp.float32)
            placed = jnp.concatenate(
                [
                    jnp.where(match, rounded, 0.0).astype(jnp.bfloat16),
                    jnp.where(match, depart - rounded, 0.0).astype(jnp.bfloat16),
                ],
                axis=0,
            )
            forcing = forcing + lax.dot_general(
                pick, placed, (((1,), (1,)), ((), ())), preferred_element_type=jnp.float32
            )
    forcing = forcing[:, :LANE] + forcing[:, LANE:]

    back = inc
    for _ in range(STEPS):
        back = step(back, coef, -1.0)

    buf[...] = jnp.zeros_like(buf)
    for t in range(TILES):
        for f in range(FIELDS):
            first = (t * FIELDS + f) * MID
            buf[f * WIN + edge : f * WIN + edge + MID, t * LANE : (t + 1) * LANE] = forcing[
                first : first + MID, :
            ]
    inject = tuple(buf[f * WIN : (f + 1) * WIN, :] for f in range(FIELDS))

    def push(state, turn):
        scale = jnp.where(obs_at == turn, 1.0, 0.0)
        return tuple(a + scale * b for a, b in zip(state, inject, strict=True))

    follows = jnp.where(lax.axis_index("tm") < TIMES - 1, 1.0, 0.0)
    adjoint = push(tuple(follows * e for e in end), STEPS)
    for turn in range(STEPS):
        adjoint = push(step(adjoint, coef, -1.0), STEPS - 1 - turn)

    for f in range(FIELDS):
        mine = slice(ROWS, 2 * ROWS)
        kinds = (inc[f][mine] + adjoint[f][mine], -end[f][mine], -back[f][mine], rates[f])
        for q, kind in enumerate(kinds):
            for t in range(TILES):
                first = (t * FIELDS * ROWS + f * ROWS) * KINDS + q
                out[pl.ds(first, ROWS, stride=KINDS), :] = kind[:, t * LANE : (t + 1) * LANE]
    used = TILES * FIELDS * ROWS * KINDS
    out[used:, :] = jnp.zeros((TIMES * KINDS - used, LANE), jnp.float32)


def time_kernel(parts, out):
    spans, length = 8, TIMES // 8
    sub = lax.broadcasted_iota(jnp.int32, (spans, LANE), 0)

    def load(q):
        return [parts[pl.ds(i * KINDS + q, spans, stride=length * KINDS), :] for i in range(length)]

    def up(x, by, fill):
        return jnp.where(sub < spans - by, pltpu.roll(x, spans - by, 0), fill)

    def down(x, by, fill):
        return jnp.where(sub >= by, pltpu.roll(x, by, 0), fill)

    x, y, z, c = (load(q) for q in range(KINDS))
    y = [down(y[-1], 1, 0.0)] + y[:-1]
    z = z[1:] + [up(z[0], 1, 0.0)]
    g = [(a + b) + d for a, b, d in zip(x, y, z, strict=True)]

    part, factor = [None] * length, [None] * length
    part[-1], factor[-1] = g[-1], jnp.ones_like(g[-1])
    for i in range(length - 2, -1, -1):
        part[i] = g[i] + c[i + 1] * part[i + 1]
        factor[i] = c[i + 1] * factor[i + 1]
    a, b = c[0] * factor[0], c[0] * part[0]
    for by in (1, 2, 4):
        a, b = a * up(a, by, 1.0), b + a * up(b, by, 0.0)
    enter = up(b, 1, 0.0)
    total = [p + f * enter for p, f in zip(part, factor, strict=True)]

    term = [(1.0 - r * r) * s for r, s in zip(c, total, strict=True)]
    part, factor = [term[0]], [c[0]]
    for i in range(1, length):
        part.append(c[i] * part[-1] + term[i])
        factor.append(c[i] * factor[-1])
    a, b = factor[-1], part[-1]
    for by in (1, 2, 4):
        a, b = a * down(a, by, 1.0), b + a * down(b, by, 0.0)
    enter = down(b, 1, 0.0)
    for i in range(length):
        out[pl.ds(i * 2, spans, stride=length * 2), :] = g[i]
        out[pl.ds(i * 2 + 1, spans, stride=length * 2), :] = part[i] + factor[i] * enter


def unpack_kernel(parts, gradient, direction):
    for e, out in enumerate((gradient, direction)):
        for f in range(FIELDS):
            for t in range(TILES):
                first = (t * FIELDS * ROWS + f * ROWS) * 2 + e
                out[f, :, t * LANE : (t + 1) * LANE] = parts[pl.ds(first, ROWS, stride=2), :]


def on_device(
    increments, correlation, coefficients, obs_cell, obs_value, obs_weight, obs_count, obs_step
):
    slots = jnp.arange(obs_cell.shape[1], dtype=jnp.int32)
    weight = jnp.where(slots < obs_count[0, 0], obs_weight[0], 0.0)
    lists = [obs_cell[0].astype(jnp.float32), obs_value[0], weight]
    obs = jnp.concatenate([part.reshape(ROWS, LANE) for part in lists], axis=1)
    mine = jnp.concatenate(
        [increments.reshape(FIELDS * ROWS, LON), coefficients.reshape(6 * ROWS, LON), obs], axis=0
    )
    packed = lax.all_gather(mine, "lat", axis=0, tiled=True)

    vmem = pl.BlockSpec(memory_space=pltpu.VMEM)
    smem = pl.BlockSpec(memory_space=pltpu.SMEM)
    limit = pltpu.CompilerParams(vmem_limit_bytes=32 * 1024 * 1024)
    sent = pl.pallas_call(
        subwindow_kernel,
        out_shape=jax.ShapeDtypeStruct((TIMES * KINDS, LANE), jnp.float32),
        in_specs=[smem, vmem, vmem],
        out_specs=vmem,
        scratch_shapes=[pltpu.VMEM((FIELDS * WIN, LON), jnp.float32)],
        compiler_params=limit,
    )(obs_step, packed, correlation[0])
    owned = lax.all_to_all(sent, "tm", 0, 0, tiled=True)
    solved = pl.pallas_call(
        time_kernel,
        out_shape=jax.ShapeDtypeStruct((TIMES * 2, LANE), jnp.float32),
        in_specs=[vmem],
        out_specs=vmem,
        compiler_params=limit,
    )(owned)
    returned = lax.all_to_all(solved, "tm", 0, 0, tiled=True)
    shape = jax.ShapeDtypeStruct((FIELDS, ROWS, LON), jnp.float32)
    gradient, direction = pl.pallas_call(
        unpack_kernel,
        out_shape=(shape, shape),
        in_specs=[vmem],
        out_specs=(vmem, vmem),
        compiler_params=limit,
    )(returned)
    return gradient[None], direction[None]


def solution(mesh):
    return jax.shard_map(
        on_device,
        mesh=mesh,
        in_specs=(
            P("tm", None, "lat", None),
            P("tm", None, "lat", None),
            P(None, "lat", None),
            P("tm", "lat"),
            P("tm", "lat"),
            P("tm", "lat"),
            P("tm", "lat"),
            P("tm"),
        ),
        out_specs=(P("tm", None, "lat", None), P("tm", None, "lat", None)),
        check_vma=False,
    )
```

profile of v0, /device:TPU:8, one launch (start us, length us, event | category | flops | bytes accessed | tf_op | source)
XLA Modules:
  0.0 72.9 jit_solution(13635052109162924475)
XLA Ops:
  1.9 0.0 copy-start.2
  1.9 0.7 convert_element_type.7
  2.6 0.0 copy-done.2
  2.6 0.0 copy-start.1
  2.7 0.7 copy-done.1
  3.3 0.9 %maximum_maximum_fusion = f32[88,384]{1,0:T(8,128)S(1)} fusion(f32[8,128]{1,0:T(8,128)S(1)} %fusion, f32[8,128]{1,0:T(8,128)S(1)} %bitcast.22, f32[8,128]{1,0:T(8,128)S(1)} %bitcast.21, f32[48,384]{1,0:T(8,128)} %bitcast.19, f32[32,384]{1,0:T(8,128)} %bitcast.20), kind=kLoop, calls=%fused_computation | loop fusion | flops 135168 | bytes 270336 | tf_op jit(solution)/shard_map/concatenate | solution.py:252
  4.2 0.0 copy-start
  4.2 7.3 %all_gather.3.packed = f32[352,384]{1,0:T(8,128)S(1)} all-gather(f32[88,384]{1,0:T(8,128)S(1)} %maximum_maximum_fusion), channel_id=1, replica_groups=mesh['tm'=128,'lat'=4] {'lat'}, dimensions={0}, use_global_device_ids=true | all-gather | bytes 675840 | tf_op jit(solution)/shard_map/all_gather | solution.py:255
  11.5 0.0 copy-done
  11.5 3.2 %shard_map.95 = f32[512,128]{1,0:T(8,128)S(1)} custom-call(s32[1]{0:T(128)S(6)} %copy.11.obs_step, f32[352,384]{1,0:T(8,128)S(1)} %all_gather.3.packed, f32[4,8,384]{2,1,0:T(8,128)S(1)} %bitcast.18), custom_call_target="tpu_custom_call" | custom-call | tf_op jit(solution)/shard_map/pallas_call | solution.py:260
  14.7 37.0 %all_to_all.22 = f32[128,4,128]{2,1,0:T(4,128)S(1)} all-to-all(f32[128,4,128]{2,1,0:T(4,128)S(1)} %bitcast.14), channel_id=1, replica_groups=mesh['tm'=128,'lat'=4] {'tm'}, dimensions={0} | all-to-all | bytes 524288 | tf_op jit(solution)/shard_map/all_to_all | solution.py:268
  51.8 0.3 shard_map.96
  52.0 20.2 %all_to_all.23 = f32[128,2,128]{2,1,0:T(2,128)S(1)} all-to-all(f32[128,2,128]{2,1,0:T(2,128)S(1)} %bitcast.16), channel_id=1, replica_groups=mesh['tm'=128,'lat'=4] {'tm'}, dimensions={0} | all-to-all | bytes 262144 | tf_op jit(solution)/shard_map/all_to_all | solution.py:276
  72.3 0.6 shard_map.97
  (1 shorter events, 0.0 us)
Async XLA Ops:
  1.9 0.7 copy-start.2
  2.6 0.7 copy-start.1
  4.2 7.3 %copy-start = (f32[1,4,8,384]{3,2,1,0:T(8,128)S(1)}, f32[1,4,8,384]{3,2,1,0:T(8,128)}, u32[]{:S(2)}) copy-start(f32[1,4,8,384]{3,2,1,0:T(8,128)} %param.9) | copy-start | bytes 147460
where the time goes:
time: 73.2 us; the launch traced here: 72.9 us
  blocking collectives  64.5 us (88%)
  Pallas kernels  4.12 us (6%)
  between operations  1.97 us (3%)
  other arithmetic  1.6 us (2%)
    all_to_all x1, blocking collectives, on_device(): owned = lax.all_to_all(sent, 'tm', 0, 0, tiled=True)  37 us
    all_to_all x1, blocking collectives, on_device(): returned = lax.all_to_all(solved, 'tm', 0, 0, tiled=True)  20.2 us
    all_gather x1, blocking collectives, on_device(): packed = lax.all_gather(mine, 'lat', axis=0, tiled=True)  7.26 us
    pallas_call x1, Pallas kernels, on_device(): pl.pallas_call(subwindow_kernel, out_shape=jax.ShapeDtypeStruct((TIMES *...  3.19 us

commit v1 on v0

--- a/solution.py
+++ b/solution.py
@@ -18,6 +18,10 @@
 PACK = 11 * ROWS
 KINDS = 4
 TIMES = 128
+SPAN = 16
+BLOCKS = TIMES // SPAN
+SHARE = FIELDS * ROWS * TILES // SPAN
+MAPS = 8
 CHUNK = 256
 
 
@@ -61,9 +65,32 @@
     return big, (value - big.astype(jnp.float32)).astype(jnp.bfloat16)
 
 
+def pack_kernel(inc, coef, cell, value, weight, count, out, cell_buf, weight_buf, sems):
+    first = (FIELDS + 6) * ROWS
+    moves = (
+        (cell, cell_buf),
+        (weight, weight_buf),
+        (coef, out.at[FIELDS * ROWS : first, :]),
+        (inc, out.at[0 : FIELDS * ROWS, :]),
+        (value, out.at[first:PACK, LANE : 2 * LANE]),
+    )
+    copies = [pltpu.make_async_copy(a, b, sems.at[i]) for i, (a, b) in enumerate(moves)]
+    for copy in copies:
+        copy.start()
+    slot = lax.broadcasted_iota(jnp.int32, (ROWS, LANE), 0) * LANE
+    slot = slot + lax.broadcasted_iota(jnp.int32, (ROWS, LANE), 1)
+    live = slot < count[0, 0]
+    for copy in copies[:2]:
+        copy.wait()
+    out[first:PACK, 0:LANE] = cell_buf[...].astype(jnp.float32)
+    out[first:PACK, 2 * LANE :] = jnp.where(live, weight_buf[...], 0.0)
+    for copy in copies[2:]:
+        copy.wait()
+
+
 def subwindow_kernel(obs_step, packed, rates, out, buf):
     slab = lax.axis_index("lat")
-    obs_at = obs_step[0]
+    obs_at = jnp.broadcast_to(obs_step[...], (WIN, LON))
 
     def window(base):
         parts = []
@@ -180,100 +207,161 @@
     for turn in range(STEPS):
         adjoint = push(step(adjoint, coef, -1.0), STEPS - 1 - turn)
 
+    mine = slice(ROWS, 2 * ROWS)
     for f in range(FIELDS):
-        mine = slice(ROWS, 2 * ROWS)
         kinds = (inc[f][mine] + adjoint[f][mine], -end[f][mine], -back[f][mine], rates[f])
+        half, odd = divmod(f, 2)
         for q, kind in enumerate(kinds):
             for t in range(TILES):
-                first = (t * FIELDS * ROWS + f * ROWS) * KINDS + q
-                out[pl.ds(first, ROWS, stride=KINDS), :] = kind[:, t * LANE : (t + 1) * LANE]
-    used = TILES * FIELDS * ROWS * KINDS
-    out[used:, :] = jnp.zeros((TIMES * KINDS - used, LANE), jnp.float32)
-
-
-def time_kernel(parts, out):
-    spans, length = 8, TIMES // 8
-    sub = lax.broadcasted_iota(jnp.int32, (spans, LANE), 0)
-
-    def load(q):
-        return [parts[pl.ds(i * KINDS + q, spans, stride=length * KINDS), :] for i in range(length)]
-
-    def up(x, by, fill):
-        return jnp.where(sub < spans - by, pltpu.roll(x, spans - by, 0), fill)
-
-    def down(x, by, fill):
-        return jnp.where(sub >= by, pltpu.roll(x, by, 0), fill)
-
-    x, y, z, c = (load(q) for q in range(KINDS))
-    y = [down(y[-1], 1, 0.0)] + y[:-1]
-    z = z[1:] + [up(z[0], 1, 0.0)]
-    g = [(a + b) + d for a, b, d in zip(x, y, z, strict=True)]
-
-    part, factor = [None] * length, [None] * length
-    part[-1], factor[-1] = g[-1], jnp.ones_like(g[-1])
-    for i in range(length - 2, -1, -1):
-        part[i] = g[i] + c[i + 1] * part[i + 1]
-        factor[i] = c[i + 1] * factor[i + 1]
-    a, b = c[0] * factor[0], c[0] * part[0]
-    for by in (1, 2, 4):
-        a, b = a * up(a, by, 1.0), b + a * up(b, by, 0.0)
-    enter = up(b, 1, 0.0)
-    total = [p + f * enter for p, f in zip(part, factor, strict=True)]
-
-    term = [(1.0 - r * r) * s for r, s in zip(c, total, strict=True)]
-    part, factor = [term[0]], [c[0]]
-    for i in range(1, length):
-        part.append(c[i] * part[-1] + term[i])
-        factor.append(c[i] * factor[-1])
-    a, b = factor[-1], part[-1]
-    for by in (1, 2, 4):
-        a, b = a * down(a, by, 1.0), b + a * down(b, by, 0.0)
-    enter = down(b, 1, 0.0)
-    for i in range(length):
-        out[pl.ds(i * 2, spans, stride=length * 2), :] = g[i]
-        out[pl.ds(i * 2 + 1, spans, stride=length * 2), :] = part[i] + factor[i] * enter
+                first = half * ROWS * KINDS * SHARE + q * SHARE + odd * TILES + t
+                out[pl.ds(first, ROWS, stride=KINDS * SHARE), :] = kind[:, t * LANE : (t + 1) * LANE]
+
+
+def load_block(parts):
+    def load(i, q):
+        first = (i * KINDS + q) * SHARE
+        return parts[first : first + SHARE, :]
+
+    x, y, z, c = ([load(i, q) for i in range(SPAN)] for q in range(KINDS))
+    g = list(x)
+    for i in range(1, SPAN):
+        g[i] = g[i] + y[i - 1]
+        g[i - 1] = g[i - 1] + z[i]
+    return g, y, z, c
+
+
+def block_kernel(parts, out):
+    g, y, z, c = load_block(parts)
+    sums, factors = [g[-1]], [jnp.ones_like(g[-1])]
+    for i in range(SPAN - 2, -1, -1):
+        sums.insert(0, g[i] + c[i + 1] * sums[0])
+        factors.insert(0, c[i + 1] * factors[0])
+    shares = [1.0 - r * r for r in c]
+    own, push = shares[0] * sums[0], shares[0] * factors[0]
+    for i in range(1, SPAN):
+        own = c[i] * own + shares[i] * sums[i]
+        push = c[i] * push + shares[i] * factors[i]
+    terms = (
+        c[0] * factors[0],
+        c[0],
+        push,
+        shares[0] * factors[0],
+        c[0] * sums[0] + z[0],
+        own,
+        y[-1],
+        z[0],
+    )
+    size = MAPS * SHARE
+    for i, term in enumerate(terms):
+        out[i * SHARE : (i + 1) * SHARE, :] = term
+    whole = out[0:size, :]
+    for b in range(1, BLOCKS):
+        out[b * size : (b + 1) * size, :] = whole
+
+
+def time_kernel(parts, maps, out):
+    block = jnp.right_shift(lax.axis_index("tm"), 4)
+
+    def term(b, i):
+        first = (b * MAPS + i) * SHARE
+        return maps[first : first + SHARE, :]
+
+    through, first_rate, push, edge, back, own, last_y, first_z = (
+        [term(b, i) for b in range(BLOCKS)] for i in range(MAPS)
+    )
+    zero = jnp.zeros_like(own[0])
+    before = [zero] + last_y[:-1]
+    after = first_z[1:] + [zero]
+    later = [zero]
+    for b in range(BLOCKS - 1, 0, -1):
+        later.insert(0, (back[b] + first_rate[b] * before[b]) + through[b] * later[0])
+    earlier = [zero]
+    for b in range(BLOCKS - 1):
+        made = (own[b] + push[b] * later[b]) + edge[b] * before[b]
+        earlier.append(made + through[b] * earlier[-1])
+
+    def mine(values):
+        picked = values[0]
+        for b in range(1, BLOCKS):
+            picked = jnp.where(block == b, values[b], picked)
+        return picked
+
+    g, _, _, c = load_block(parts)
+    g[0] = g[0] + mine(before)
+    total = [g[-1] + mine(later)]
+    g[-1] = g[-1] + mine(after)
+    for i in range(SPAN - 2, -1, -1):
+        total.insert(0, g[i] + c[i + 1] * total[0])
+    smooth = mine(earlier)
+    for i in range(SPAN):
+        smooth = c[i] * smooth + (1.0 - c[i] * c[i]) * total[i]
+        for e, value in enumerate((g[i], smooth)):
+            first = (i * 2 + e) * SHARE
+            out[first : first + SHARE, :] = value
 
 
 def unpack_kernel(parts, gradient, direction):
     for e, out in enumerate((gradient, direction)):
         for f in range(FIELDS):
+            half, odd = divmod(f, 2)
             for t in range(TILES):
-                first = (t * FIELDS * ROWS + f * ROWS) * 2 + e
-                out[f, :, t * LANE : (t + 1) * LANE] = parts[pl.ds(first, ROWS, stride=2), :]
+                first = half * ROWS * 2 * SHARE + e * SHARE + odd * TILES + t
+                out[f, :, t * LANE : (t + 1) * LANE] = parts[pl.ds(first, ROWS, stride=2 * SHARE), :]
 
 
 def on_device(
     increments, correlation, coefficients, obs_cell, obs_value, obs_weight, obs_count, obs_step
 ):
-    slots = jnp.arange(obs_cell.shape[1], dtype=jnp.int32)
-    weight = jnp.where(slots < obs_count[0, 0], obs_weight[0], 0.0)
-    lists = [obs_cell[0].astype(jnp.float32), obs_value[0], weight]
-    obs = jnp.concatenate([part.reshape(ROWS, LANE) for part in lists], axis=1)
-    mine = jnp.concatenate(
-        [increments.reshape(FIELDS * ROWS, LON), coefficients.reshape(6 * ROWS, LON), obs], axis=0
+    vmem = pl.BlockSpec(memory_space=pltpu.VMEM)
+    far = pl.BlockSpec(memory_space=pltpu.HBM)
+    limit = pltpu.CompilerParams(vmem_limit_bytes=32 * 1024 * 1024)
+    mine = pl.pallas_call(
+        pack_kernel,
+        out_shape=jax.ShapeDtypeStruct((PACK, LON), jnp.float32),
+        in_specs=[far] * 5 + [pl.BlockSpec(memory_space=pltpu.SMEM)],
+        out_specs=vmem,
+        scratch_shapes=[
+            pltpu.VMEM((ROWS, LANE), jnp.int32),
+            pltpu.VMEM((ROWS, LANE), jnp.float32),
+            pltpu.SemaphoreType.DMA((5,)),
+        ],
+        compiler_params=pltpu.CompilerParams(vmem_limit_bytes=60 * 1024 * 1024),
+    )(
+        increments.reshape(FIELDS * ROWS, LON),
+        coefficients.reshape(6 * ROWS, LON),
+        obs_cell.reshape(ROWS, LANE),
+        obs_value.reshape(ROWS, LANE),
+        obs_weight.reshape(ROWS, LANE),
+        obs_count,
     )
     packed = lax.all_gather(mine, "lat", axis=0, tiled=True)
-
-    vmem = pl.BlockSpec(memory_space=pltpu.VMEM)
-    smem = pl.BlockSpec(memory_space=pltpu.SMEM)
-    limit = pltpu.CompilerParams(vmem_limit_bytes=32 * 1024 * 1024)
+    spans = [list(range(first, first + SPAN)) for first in range(0, TIMES, SPAN)]
+    strides = [list(range(first, TIMES, SPAN)) for first in range(SPAN)]
     sent = pl.pallas_call(
         subwindow_kernel,
-        out_shape=jax.ShapeDtypeStruct((TIMES * KINDS, LANE), jnp.float32),
-        in_specs=[smem, vmem, vmem],
+        out_shape=jax.ShapeDtypeStruct((SPAN * KINDS * SHARE, LANE), jnp.float32),
+        in_specs=[vmem] * 3,
         out_specs=vmem,
         scratch_shapes=[pltpu.VMEM((FIELDS * WIN, LON), jnp.float32)],
         compiler_params=limit,
-    )(obs_step, packed, correlation[0])
-    owned = lax.all_to_all(sent, "tm", 0, 0, tiled=True)
-    solved = pl.pallas_call(
-        time_kernel,
-        out_shape=jax.ShapeDtypeStruct((TIMES * 2, LANE), jnp.float32),
+    )(obs_step.reshape(1, 1), packed, correlation[0])
+    owned = lax.all_to_all(sent, "tm", 0, 0, axis_index_groups=spans, tiled=True)
+    reduced = pl.pallas_call(
+        block_kernel,
+        out_shape=jax.ShapeDtypeStruct((BLOCKS * MAPS * SHARE, LANE), jnp.float32),
         in_specs=[vmem],
         out_specs=vmem,
         compiler_params=limit,
     )(owned)
-    returned = lax.all_to_all(solved, "tm", 0, 0, tiled=True)
+    maps = lax.all_to_all(reduced, "tm", 0, 0, axis_index_groups=strides, tiled=True)
+    solved = pl.pallas_call(
+        time_kernel,
+        out_shape=jax.ShapeDtypeStruct((SPAN * 2 * SHARE, LANE), jnp.float32),
+        in_specs=[vmem] * 2,
+        out_specs=vmem,
+        compiler_params=limit,
+    )(owned, maps)
+    returned = lax.all_to_all(solved, "tm", 0, 0, axis_index_groups=spans, tiled=True)
     shape = jax.ShapeDtypeStruct((FIELDS, ROWS, LON), jnp.float32)
     gradient, direction = pl.pallas_call(
         unpack_kernel,

time: 73.2 us -> 69.7 us (0.952)
  blocking collectives: 64.5 us -> 61.8 us
  other arithmetic: 1.6 us -> 0 us
  Pallas kernels: 4.12 us -> 5.65 us
    all_to_all x2 -> x3, blocking collectives: 57.3 us -> 54.3 us  [the longest x1 22.2 us: on_device(): lax.all_to_all(reduced, 'tm', 0, 0, axis_index_groups=strides, tiled=True)]
    pallas_call x2 -> x4, Pallas kernels: 3.47 us -> 5 us  [the longest x1 3.21 us: on_device(): pl.pallas_call(subwindow_kernel, out_shape=jax.ShapeDtypeStruct((SPAN * K...]
    concatenate x1 -> x0, other arithmetic: 0.9 us -> none  [on_device(): jnp.concatenate([increments.reshape(FIELDS * ROWS, LON), coefficients.res...]
where the time goes in v1:
time: 69.7 us; the launch traced here: 69.4 us
  blocking collectives  61.8 us (89%)
  Pallas kernels  5.65 us (8%)
  between operations  1.96 us (3%)
    all_to_all x1, blocking collectives, on_device(): lax.all_to_all(reduced, 'tm', 0, 0, axis_index_groups=strides, tiled=True)  22.2 us
    all_to_all x1, blocking collectives, on_device(): lax.all_to_all(sent, 'tm', 0, 0, axis_index_groups=spans, tiled=True)  18.7 us
    all_to_all x1, blocking collectives, on_device(): lax.all_to_all(solved, 'tm', 0, 0, axis_index_groups=spans, tiled=True)  13.4 us
    all_gather x1, blocking collectives, on_device(): packed = lax.all_gather(mine, 'lat', axis=0, tiled=True)  7.47 us
    pallas_call x1, Pallas kernels, on_device(): pl.pallas_call(subwindow_kernel, out_shape=jax.ShapeDtypeStruct((SPAN * K...  3.21 us
    pallas_call x1, Pallas kernels, on_device(): pl.pallas_call(pack_kernel, out_shape=jax.ShapeDtypeStruct((PACK, LON), j...  1.61 us

profile of v1, /device:TPU:8, one launch (start us, length us, event | category | flops | bytes accessed | tf_op | source)
XLA Modules:
  0.0 69.4 jit_solution(7634802428774080775)
XLA Ops:
  1.9 1.6 %shard_map.95 = f32[88,384]{1,0:T(8,128)} custom-call(f32[32,384]{1,0:T(8,128)} %bitcast.21, f32[48,384]{1,0:T(8,128)} %bitcast.20, s32[8,128]{1,0:T(8,128)} %bitcast.22, f32[8,128]{1,0:T(8,128)} %bitcast.23, f32[8,128]{1,0:T(8,128)} %bitcast.24, s32[1,1]{1,0:T(1,128)S(6)} %copy.10.count), custom_call_target="tpu_custom_call" | custom-call | tf_op jit(solution)/shard_map/pallas_call | solution.py:318
  3.5 0.0 copy-start
  3.6 7.5 %all_gather.3.packed = f32[352,384]{1,0:T(8,128)S(1)} all-gather(f32[88,384]{1,0:T(8,128)} %shard_map.95), channel_id=1, replica_groups=mesh['tm'=128,'lat'=4] {'lat'}, dimensions={0}, use_global_device_ids=true | all-gather | bytes 675840 | tf_op jit(solution)/shard_map/all_gather | solution.py:337
  11.0 0.0 copy-done
  11.0 3.2 %shard_map.96 = f32[384,128]{1,0:T(8,128)S(1)} custom-call(s32[1,1]{1,0:T(1,128)} %bitcast.13.obs_step, f32[352,384]{1,0:T(8,128)S(1)} %all_gather.3.packed, f32[4,8,384]{2,1,0:T(8,128)S(1)} %bitcast.19), custom_call_target="tpu_custom_call" | custom-call | tf_op jit(solution)/shard_map/pallas_call | solution.py:340
  14.3 18.7 %all_to_all.33 = f32[16,24,128]{2,1,0:T(8,128)S(1)} all-to-all(f32[16,24,128]{2,1,0:T(8,128)S(1)} %bitcast.17), channel_id=1, replica_groups={{0,4,8,12,16,20,24,28,32,36,40,44,48,52,56,60},{64,68,72,76,80,84,88,92..., dimensions={0} | all-to-all | bytes 393216 | tf_op jit(solution)/shard_map/all_to_all | solution.py:348
  32.9 0.1 shard_map.97
  33.0 22.2 %all_to_all.34 = f32[8,48,128]{2,1,0:T(8,128)S(1)} all-to-all(f32[8,48,128]{2,1,0:T(8,128)S(1)} %bitcast.16), channel_id=1, replica_groups={{0,64,128,192,256,320,384,448},{4,68,132,196,260,324,388,452},{8,72,136..., dimensions={0} | all-to-all | bytes 393216 | tf_op jit(solution)/shard_map/all_to_all | solution.py:356
  55.2 0.1 shard_map.98
  55.3 13.4 %all_to_all.35 = f32[16,12,128]{2,1,0:T(8,128)S(1)} all-to-all(f32[16,12,128]{2,1,0:T(8,128)S(1)} %all_to_all.27), channel_id=1, replica_groups={{0,4,8,12,16,20,24,28,32,36,40,44,48,52,56,60},{64,68,72,76,80,84,88,92..., dimensions={0} | all-to-all | bytes 196608 | tf_op jit(solution)/shard_map/all_to_all | solution.py:364
  68.8 0.6 shard_map.99
  (2 shorter events, 0.0 us)
Async XLA Ops:
  3.5 7.5 %copy-start = (f32[1,4,8,384]{3,2,1,0:T(8,128)S(1)}, f32[1,4,8,384]{3,2,1,0:T(8,128)}, u32[]{:S(2)}) copy-start(f32[1,4,8,384]{3,2,1,0:T(8,128)} %param.9) | copy-start | bytes 147460

commit v2 on v1

--- a/solution.py
+++ b/solution.py
@@ -22,7 +22,7 @@
 BLOCKS = TIMES // SPAN
 SHARE = FIELDS * ROWS * TILES // SPAN
 MAPS = 8
-CHUNK = 256
+CHUNK = 512
 
 
 def lon_roll(field, by):
@@ -30,7 +30,7 @@
 
 
 def row_roll(field, by):
-    return pltpu.roll(field, by % WIN, 0)
+    return pltpu.roll(field, by % field.shape[0], 0)
 
 
 def step(state, coef, sign):
@@ -88,7 +88,7 @@
         copy.wait()
 
 
-def subwindow_kernel(obs_step, packed, rates, out, buf):
+def subwindow_kernel(obs_step, packed, rates, out):
     slab = lax.axis_index("lat")
     obs_at = jnp.broadcast_to(obs_step[...], (WIN, LON))
 
@@ -128,22 +128,25 @@
             seen = tuple(jnp.where(obs_at == turn + 1, a, b) for a, b in zip(state, seen, strict=True))
     end = state
 
-    for f in range(FIELDS):
-        buf[f * WIN : (f + 1) * WIN, :] = seen[f]
-    edge = (WIN - MID) // 2
+    upper = lax.broadcasted_iota(jnp.int32, (ROWS, LON), 0) < ROWS // 2
+
+    def fold(x):
+        ends = jnp.where(upper, x[2 * ROWS :], x[:ROWS])
+        return jnp.concatenate([x[ROWS : 2 * ROWS], ends], axis=0)
+
+    inc, end, seen = (tuple(fold(x) for x in fields) for fields in (inc, end, seen))
+    coef = {name: tuple(fold(x) for x in coef[name]) for name in ("common", "backward")}
     table = jnp.concatenate(
-        [
-            buf[f * WIN + edge : f * WIN + edge + MID, t * LANE : (t + 1) * LANE]
-            for t in range(TILES)
-            for f in range(FIELDS)
-        ],
-        axis=0,
+        [seen[f][:, t * LANE : (t + 1) * LANE] for t in range(TILES) for f in range(FIELDS)], axis=0
     )
     high = table.shape[0]
-    table_parts = jnp.concatenate(split(table), axis=1)
-
-    hi_iota = lax.broadcasted_iota(jnp.int32, (high, LANE), 0)
-    lo_iota = lax.broadcasted_iota(jnp.int32, (LANE, LANE), 0)
+    table_parts = jnp.concatenate(split(jnp.transpose(table)), axis=0)
+
+    half = jnp.bfloat16
+    hi_iota = lax.broadcasted_iota(jnp.int32, (high, CHUNK), 0).astype(half)
+    lo_iota = lax.broadcasted_iota(jnp.int32, (LANE, CHUNK), 0)
+    lo_half = lo_iota.astype(half)
+    one, none = jnp.ones((high, CHUNK), half), jnp.zeros((high, CHUNK), half)
     forcing = jnp.zeros((high, 2 * LANE), jnp.float32)
     for owner in range(SLABS):
         base = owner * PACK + 10 * ROWS
@@ -155,30 +158,29 @@
         field_row = jnp.right_shift(tile_row * 21846, 16)
         tile = tile_row - field_row * TILES
         field = jnp.right_shift(field_row, 5)
-        rel = jnp.bitwise_and(field_row, NY - 1) - (slab * ROWS - edge)
-        near = jnp.logical_and(rel >= 0, rel < MID)
-        spot = jnp.where(near, tile * (FIELDS * MID) + field * MID + rel, -1)
-        for pair in range(ROWS // 2):
-            rows = (2 * pair, 2 * pair + 1)
-            pick = jnp.concatenate(
-                [jnp.where(hi_iota == spot[r : r + 1, :], 1.0, 0.0) for r in rows], axis=1
-            ).astype(jnp.bfloat16)
-            match = jnp.concatenate([lo_iota == low[r : r + 1, :] for r in rows], axis=1)
+        rel = jnp.bitwise_and(field_row, NY - 1) - slab * ROWS
+        near = jnp.logical_and(rel >= -(ROWS // 2), rel < ROWS + ROWS // 2)
+        place = tile * (FIELDS * MID) + field * MID + jnp.bitwise_and(rel, MID - 1)
+        spot = jnp.where(near, place, -1)
+        for pair in range(ROWS // 4):
+            rows = tuple(range(4 * pair, 4 * pair + 4))
+            def wide(x):
+                return jnp.concatenate([x[r : r + 1, :] for r in rows], axis=1)
+
+            here, column = wide(spot), wide(low)
+            pick = jnp.where(hi_iota == here.astype(half), one, none)
+            match = lo_iota == column
+            match_half = lo_half == column.astype(half)
             columns = lax.dot_general(
-                table_parts, pick, (((0,), (0,)), ((), ())), preferred_element_type=jnp.float32
+                table_parts, pick, (((1,), (0,)), ((), ())), preferred_element_type=jnp.float32
             )
             columns = columns[:LANE] + columns[LANE:]
             sampled = jnp.sum(jnp.where(match, columns, 0.0), axis=0, keepdims=True)
-            wide_value = jnp.concatenate([value[r : r + 1, :] for r in rows], axis=1)
-            wide_weight = jnp.concatenate([weight[r : r + 1, :] for r in rows], axis=1)
-            depart = wide_weight * (sampled - wide_value)
-            rounded = depart.astype(jnp.bfloat16).astype(jnp.float32)
+            depart = wide(weight) * (sampled - wide(value))
+            big = depart.astype(half)
+            small = (depart - big.astype(jnp.float32)).astype(half)
             placed = jnp.concatenate(
-                [
-                    jnp.where(match, rounded, 0.0).astype(jnp.bfloat16),
-                    jnp.where(match, depart - rounded, 0.0).astype(jnp.bfloat16),
-                ],
-                axis=0,
+                [jnp.where(match_half, part, none[:LANE]) for part in (big, small)], axis=0
             )
             forcing = forcing + lax.dot_general(
                 pick, placed, (((1,), (1,)), ((), ())), preferred_element_type=jnp.float32
@@ -189,17 +191,19 @@
     for _ in range(STEPS):
         back = step(back, coef, -1.0)
 
-    buf[...] = jnp.zeros_like(buf)
-    for t in range(TILES):
-        for f in range(FIELDS):
-            first = (t * FIELDS + f) * MID
-            buf[f * WIN + edge : f * WIN + edge + MID, t * LANE : (t + 1) * LANE] = forcing[
-                first : first + MID, :
-            ]
-    inject = tuple(buf[f * WIN : (f + 1) * WIN, :] for f in range(FIELDS))
+    inject = tuple(
+        jnp.concatenate(
+            [
+                forcing[(t * FIELDS + f) * MID : (t * FIELDS + f + 1) * MID, :]
+                for t in range(TILES)
+            ],
+            axis=1,
+        )
+        for f in range(FIELDS)
+    )
 
     def push(state, turn):
-        scale = jnp.where(obs_at == turn, 1.0, 0.0)
+        scale = jnp.where(obs_at[:MID] == turn, 1.0, 0.0)
         return tuple(a + scale * b for a, b in zip(state, inject, strict=True))
 
     follows = jnp.where(lax.axis_index("tm") < TIMES - 1, 1.0, 0.0)
@@ -207,7 +211,7 @@
     for turn in range(STEPS):
         adjoint = push(step(adjoint, coef, -1.0), STEPS - 1 - turn)
 
-    mine = slice(ROWS, 2 * ROWS)
+    mine = slice(0, ROWS)
     for f in range(FIELDS):
         kinds = (inc[f][mine] + adjoint[f][mine], -end[f][mine], -back[f][mine], rates[f])
         half, odd = divmod(f, 2)
@@ -342,7 +346,6 @@
         out_shape=jax.ShapeDtypeStruct((SPAN * KINDS * SHARE, LANE), jnp.float32),
         in_specs=[vmem] * 3,
         out_specs=vmem,
-        scratch_shapes=[pltpu.VMEM((FIELDS * WIN, LON), jnp.float32)],
         compiler_params=limit,
     )(obs_step.reshape(1, 1), packed, correlation[0])
     owned = lax.all_to_all(sent, "tm", 0, 0, axis_index_groups=spans, tiled=True)

time: 69.7 us -> 69.1 us (level)
  no operation moved by 1% of the time
where the time goes in v2:
time: 69.1 us; the launch traced here: 68.8 us
  blocking collectives  61.8 us (89%)
  Pallas kernels  5.05 us (7%)
  between operations  1.96 us (3%)
    all_to_all x1, blocking collectives, on_device(): lax.all_to_all(reduced, 'tm', 0, 0, axis_index_groups=strides, tiled=True)  22.1 us
    all_to_all x1, blocking collectives, on_device(): lax.all_to_all(sent, 'tm', 0, 0, axis_index_groups=spans, tiled=True)  18.7 us
    all_to_all x1, blocking collectives, on_device(): lax.all_to_all(solved, 'tm', 0, 0, axis_index_groups=spans, tiled=True)  13.5 us
    all_gather x1, blocking collectives, on_device(): packed = lax.all_gather(mine, 'lat', axis=0, tiled=True)  7.47 us
    pallas_call x1, Pallas kernels, on_device(): pl.pallas_call(subwindow_kernel, out_shape=jax.ShapeDtypeStruct((SPAN * K...  2.62 us
    pallas_call x1, Pallas kernels, on_device(): pl.pallas_call(pack_kernel, out_shape=jax.ShapeDtypeStruct((PACK, LON), j...  1.61 us

profile of v2, /device:TPU:8, one launch (start us, length us, event | category | flops | bytes accessed | tf_op | source)
XLA Modules:
  0.0 68.8 jit_solution(14963489712602677303)
XLA Ops:
  1.9 1.6 %shard_map.95 = f32[88,384]{1,0:T(8,128)} custom-call(f32[32,384]{1,0:T(8,128)} %bitcast.21, f32[48,384]{1,0:T(8,128)} %bitcast.20, s32[8,128]{1,0:T(8,128)} %bitcast.22, f32[8,128]{1,0:T(8,128)} %bitcast.23, f32[8,128]{1,0:T(8,128)} %bitcast.24, s32[1,1]{1,0:T(1,128)S(6)} %copy.10.count), custom_call_target="tpu_custom_call" | custom-call | tf_op jit(solution)/shard_map/pallas_call | solution.py:322
  3.5 0.0 copy-start
  3.6 7.5 %all_gather.3.packed = f32[352,384]{1,0:T(8,128)S(1)} all-gather(f32[88,384]{1,0:T(8,128)} %shard_map.95), channel_id=1, replica_groups=mesh['tm'=128,'lat'=4] {'lat'}, dimensions={0}, use_global_device_ids=true | all-gather | bytes 675840 | tf_op jit(solution)/shard_map/all_gather | solution.py:341
  11.0 0.0 copy-done
  11.0 2.6 %shard_map.96 = f32[384,128]{1,0:T(8,128)S(1)} custom-call(s32[1,1]{1,0:T(1,128)} %bitcast.13.obs_step, f32[352,384]{1,0:T(8,128)S(1)} %all_gather.3.packed, f32[4,8,384]{2,1,0:T(8,128)S(1)} %bitcast.19), custom_call_target="tpu_custom_call" | custom-call | tf_op jit(solution)/shard_map/pallas_call | solution.py:344
  13.7 18.7 %all_to_all.33 = f32[16,24,128]{2,1,0:T(8,128)S(1)} all-to-all(f32[16,24,128]{2,1,0:T(8,128)S(1)} %bitcast.17), channel_id=1, replica_groups={{0,4,8,12,16,20,24,28,32,36,40,44,48,52,56,60},{64,68,72,76,80,84,88,92..., dimensions={0} | all-to-all | bytes 393216 | tf_op jit(solution)/shard_map/all_to_all | solution.py:351
  32.3 0.1 shard_map.97
  32.4 22.1 %all_to_all.34 = f32[8,48,128]{2,1,0:T(8,128)S(1)} all-to-all(f32[8,48,128]{2,1,0:T(8,128)S(1)} %bitcast.16), channel_id=1, replica_groups={{0,64,128,192,256,320,384,448},{4,68,132,196,260,324,388,452},{8,72,136..., dimensions={0} | all-to-all | bytes 393216 | tf_op jit(solution)/shard_map/all_to_all | solution.py:359
  54.5 0.1 shard_map.98
  54.6 13.5 %all_to_all.35 = f32[16,12,128]{2,1,0:T(8,128)S(1)} all-to-all(f32[16,12,128]{2,1,0:T(8,128)S(1)} %all_to_all.27), channel_id=1, replica_groups={{0,4,8,12,16,20,24,28,32,36,40,44,48,52,56,60},{64,68,72,76,80,84,88,92..., dimensions={0} | all-to-all | bytes 196608 | tf_op jit(solution)/shard_map/all_to_all | solution.py:367
  68.2 0.6 shard_map.99
  (2 shorter events, 0.0 us)
Async XLA Ops:
  3.5 7.5 %copy-start = (f32[1,4,8,384]{3,2,1,0:T(8,128)S(1)}, f32[1,4,8,384]{3,2,1,0:T(8,128)}, u32[]{:S(2)}) copy-start(f32[1,4,8,384]{3,2,1,0:T(8,128)} %param.9) | copy-start | bytes 147460

commit v3 on v2

--- a/solution.py
+++ b/solution.py
@@ -329,13 +329,18 @@
             pltpu.VMEM((ROWS, LANE), jnp.float32),
             pltpu.SemaphoreType.DMA((5,)),
         ],
-        compiler_params=pltpu.CompilerParams(vmem_limit_bytes=60 * 1024 * 1024),
+        compiler_params=limit,
     )(
-        increments.reshape(FIELDS * ROWS, LON),
-        coefficients.reshape(6 * ROWS, LON),
-        obs_cell.reshape(ROWS, LANE),
-        obs_value.reshape(ROWS, LANE),
-        obs_weight.reshape(ROWS, LANE),
+        *(
+            pltpu.with_memory_space_constraint(part, pltpu.HBM)
+            for part in (
+                increments.reshape(FIELDS * ROWS, LON),
+                coefficients.reshape(6 * ROWS, LON),
+                obs_cell.reshape(ROWS, LANE),
+                obs_value.reshape(ROWS, LANE),
+                obs_weight.reshape(ROWS, LANE),
+            )
+        ),
         obs_count,
     )
     packed = lax.all_gather(mine, "lat", axis=0, tiled=True)

time: 69.1 us -> 68.3 us (0.988)
  no operation moved by 1% of the time
where the time goes in v3:
time: 68.3 us; the launch traced here: 67.9 us
  blocking collectives  61.6 us (90%)
  Pallas kernels  4.41 us (6%)
  between operations  1.96 us (3%)
    all_to_all x1, blocking collectives, on_device(): lax.all_to_all(reduced, 'tm', 0, 0, axis_index_groups=strides, tiled=True)  22.1 us
    all_to_all x1, blocking collectives, on_device(): lax.all_to_all(sent, 'tm', 0, 0, axis_index_groups=spans, tiled=True)  18.7 us
    all_to_all x1, blocking collectives, on_device(): lax.all_to_all(solved, 'tm', 0, 0, axis_index_groups=spans, tiled=True)  13.5 us
    all_gather x1, blocking collectives, on_device(): packed = lax.all_gather(mine, 'lat', axis=0, tiled=True)  7.26 us
    pallas_call x1, Pallas kernels, on_device(): pl.pallas_call(subwindow_kernel, out_shape=jax.ShapeDtypeStruct((SPAN * K...  2.62 us

profile of v3, /device:TPU:8, one launch (start us, length us, event | category | flops | bytes accessed | tf_op | source)
XLA Modules:
  0.0 67.9 jit_solution(14632836853092717500)
XLA Ops:
  1.9 1.0 %shard_map.95 = f32[88,384]{1,0:T(8,128)S(1)} custom-call(f32[32,384]{1,0:T(8,128)} %bitcast.21, f32[48,384]{1,0:T(8,128)} %bitcast.20, s32[8,128]{1,0:T(8,128)} %bitcast.22, f32[8,128]{1,0:T(8,128)} %bitcast.23, f32[8,128]{1,0:T(8,128)} %bitcast.24, s32[1,1]{1,0:T(1,128)S(6)} %copy.10.count), custom_call_target="tpu_custom_call" | custom-call | tf_op jit(solution)/shard_map/pallas_call | solution.py:322
  2.9 0.0 copy-start
  2.9 7.3 %all_gather.3.packed = f32[352,384]{1,0:T(8,128)S(1)} all-gather(f32[88,384]{1,0:T(8,128)S(1)} %shard_map.95), channel_id=1, replica_groups=mesh['tm'=128,'lat'=4] {'lat'}, dimensions={0}, use_global_device_ids=true | all-gather | bytes 675840 | tf_op jit(solution)/shard_map/all_gather | solution.py:346
  10.2 0.0 copy-done
  10.2 2.6 %shard_map.96 = f32[384,128]{1,0:T(8,128)S(1)} custom-call(s32[1,1]{1,0:T(1,128)} %bitcast.13.obs_step, f32[352,384]{1,0:T(8,128)S(1)} %all_gather.3.packed, f32[4,8,384]{2,1,0:T(8,128)S(1)} %bitcast.19), custom_call_target="tpu_custom_call" | custom-call | tf_op jit(solution)/shard_map/pallas_call | solution.py:349
  12.8 18.7 %all_to_all.33 = f32[16,24,128]{2,1,0:T(8,128)S(1)} all-to-all(f32[16,24,128]{2,1,0:T(8,128)S(1)} %bitcast.17), channel_id=1, replica_groups={{0,4,8,12,16,20,24,28,32,36,40,44,48,52,56,60},{64,68,72,76,80,84,88,92..., dimensions={0} | all-to-all | bytes 393216 | tf_op jit(solution)/shard_map/all_to_all | solution.py:356
  31.5 0.1 shard_map.97
  31.5 22.1 %all_to_all.34 = f32[8,48,128]{2,1,0:T(8,128)S(1)} all-to-all(f32[8,48,128]{2,1,0:T(8,128)S(1)} %bitcast.16), channel_id=1, replica_groups={{0,64,128,192,256,320,384,448},{4,68,132,196,260,324,388,452},{8,72,136..., dimensions={0} | all-to-all | bytes 393216 | tf_op jit(solution)/shard_map/all_to_all | solution.py:364
  53.7 0.1 shard_map.98
  53.8 13.5 %all_to_all.35 = f32[16,12,128]{2,1,0:T(8,128)S(1)} all-to-all(f32[16,12,128]{2,1,0:T(8,128)S(1)} %all_to_all.27), channel_id=1, replica_groups={{0,4,8,12,16,20,24,28,32,36,40,44,48,52,56,60},{64,68,72,76,80,84,88,92..., dimensions={0} | all-to-all | bytes 196608 | tf_op jit(solution)/shard_map/all_to_all | solution.py:372
  67.3 0.6 shard_map.99
  (2 shorter events, 0.0 us)
Async XLA Ops:
  2.9 7.3 %copy-start = (f32[1,4,8,384]{3,2,1,0:T(8,128)S(1)}, f32[1,4,8,384]{3,2,1,0:T(8,128)}, u32[]{:S(2)}) copy-start(f32[1,4,8,384]{3,2,1,0:T(8,128)} %param.9) | copy-start | bytes 147460

commit v4 on v3

--- a/solution.py
+++ b/solution.py
@@ -21,7 +21,8 @@
 SPAN = 16
 BLOCKS = TIMES // SPAN
 SHARE = FIELDS * ROWS * TILES // SPAN
-MAPS = 8
+MAPS = 6
+MAP_ROWS = MAPS * SHARE
 CHUNK = 512
 
 
@@ -147,7 +148,7 @@
     lo_iota = lax.broadcasted_iota(jnp.int32, (LANE, CHUNK), 0)
     lo_half = lo_iota.astype(half)
     one, none = jnp.ones((high, CHUNK), half), jnp.zeros((high, CHUNK), half)
-    forcing = jnp.zeros((high, 2 * LANE), jnp.float32)
+    picks, places = [], []
     for owner in range(SLABS):
         base = owner * PACK + 10 * ROWS
         cell = packed[base : base + ROWS, 0:LANE].astype(jnp.int32)
@@ -182,9 +183,14 @@
             placed = jnp.concatenate(
                 [jnp.where(match_half, part, none[:LANE]) for part in (big, small)], axis=0
             )
-            forcing = forcing + lax.dot_general(
-                pick, placed, (((1,), (1,)), ((), ())), preferred_element_type=jnp.float32
-            )
+            picks.append(pick)
+            places.append(placed)
+    forcing = lax.dot_general(
+        jnp.concatenate(picks, axis=1),
+        jnp.concatenate(places, axis=1),
+        (((1,), (1,)), ((), ())),
+        preferred_element_type=jnp.float32,
+    )
     forcing = forcing[:, :LANE] + forcing[:, LANE:]
 
     back = inc
@@ -245,43 +251,40 @@
     for i in range(1, SPAN):
         own = c[i] * own + shares[i] * sums[i]
         push = c[i] * push + shares[i] * factors[i]
-    terms = (
-        c[0] * factors[0],
-        c[0],
-        push,
-        shares[0] * factors[0],
-        c[0] * sums[0] + z[0],
-        own,
-        y[-1],
-        z[0],
-    )
-    size = MAPS * SHARE
+    block = jnp.right_shift(lax.axis_index("tm"), 4)
+    terms = (factors[0], c[0], c[0] * sums[0] + z[0], y[-1], push, own)
     for i, term in enumerate(terms):
         out[i * SHARE : (i + 1) * SHARE, :] = term
-    whole = out[0:size, :]
-    for b in range(1, BLOCKS):
-        out[b * size : (b + 1) * size, :] = whole
+    whole = out[0:MAP_ROWS, :]
+    for b in range(BLOCKS):
+        first = b * MAP_ROWS
+        if b > 0:
+            out[first : first + MAP_ROWS, :] = whole
+        first += 4 * SHARE
+        out[first : first + SHARE, :] = jnp.where(b < block, z[0], push)
 
 
 def time_kernel(parts, maps, out):
     block = jnp.right_shift(lax.axis_index("tm"), 4)
 
     def term(b, i):
-        first = (b * MAPS + i) * SHARE
+        first = b * MAP_ROWS + i * SHARE
         return maps[first : first + SHARE, :]
 
-    through, first_rate, push, edge, back, own, last_y, first_z = (
+    factor, first_rate, back, last_y, shared, own = (
         [term(b, i) for b in range(BLOCKS)] for i in range(MAPS)
     )
+    through = [r * f for r, f in zip(first_rate, factor, strict=True)]
+    edge = [(1.0 - r * r) * f for r, f in zip(first_rate, factor, strict=True)]
     zero = jnp.zeros_like(own[0])
     before = [zero] + last_y[:-1]
-    after = first_z[1:] + [zero]
+    after = shared[1:] + [zero]
     later = [zero]
     for b in range(BLOCKS - 1, 0, -1):
         later.insert(0, (back[b] + first_rate[b] * before[b]) + through[b] * later[0])
     earlier = [zero]
     for b in range(BLOCKS - 1):
-        made = (own[b] + push[b] * later[b]) + edge[b] * before[b]
+        made = (own[b] + shared[b] * later[b]) + edge[b] * before[b]
         earlier.append(made + through[b] * earlier[-1])
 
     def mine(values):
@@ -356,20 +359,22 @@
     owned = lax.all_to_all(sent, "tm", 0, 0, axis_index_groups=spans, tiled=True)
     reduced = pl.pallas_call(
         block_kernel,
-        out_shape=jax.ShapeDtypeStruct((BLOCKS * MAPS * SHARE, LANE), jnp.float32),
+        out_shape=jax.ShapeDtypeStruct((BLOCKS * MAP_ROWS, LANE), jnp.float32),
         in_specs=[vmem],
         out_specs=vmem,
         compiler_params=limit,
     )(owned)
-    maps = lax.all_to_all(reduced, "tm", 0, 0, axis_index_groups=strides, tiled=True)
+    quarters = reduced.reshape(BLOCKS, -1, 4, LANE)
+    maps = lax.all_to_all(quarters, "tm", 0, 0, axis_index_groups=strides, tiled=True)
     solved = pl.pallas_call(
         time_kernel,
         out_shape=jax.ShapeDtypeStruct((SPAN * 2 * SHARE, LANE), jnp.float32),
         in_specs=[vmem] * 2,
         out_specs=vmem,
         compiler_params=limit,
-    )(owned, maps)
-    returned = lax.all_to_all(solved, "tm", 0, 0, axis_index_groups=spans, tiled=True)
+    )(owned, maps.reshape(BLOCKS * MAP_ROWS, LANE))
+    quarters = solved.reshape(SPAN, -1, 4, LANE)
+    returned = lax.all_to_all(quarters, "tm", 0, 0, axis_index_groups=spans, tiled=True)
     shape = jax.ShapeDtypeStruct((FIELDS, ROWS, LON), jnp.float32)
     gradient, direction = pl.pallas_call(
         unpack_kernel,
@@ -377,7 +382,7 @@
         in_specs=[vmem],
         out_specs=(vmem, vmem),
         compiler_params=limit,
-    )(returned)
+    )(returned.reshape(SPAN * 2 * SHARE, LANE))
     return gradient[None], direction[None]
 
 

time: 68.3 us -> 67 us (0.981)
  blocking collectives: 61.6 us -> 60.4 us
    all_to_all x2, blocking collectives: 35.6 us -> 34.5 us  [the longest x1 22 us: on_device(): lax.all_to_all(quarters, 'tm', 0, 0, axis_index_groups=strides, tiled=True)]
where the time goes in v4:
time: 67 us; the launch traced here: 66.7 us
  blocking collectives  60.4 us (90%)
  Pallas kernels  4.36 us (7%)
  between operations  1.95 us (3%)
    all_to_all x1, blocking collectives, on_device(): lax.all_to_all(quarters, 'tm', 0, 0, axis_index_groups=strides, tiled=True)  22 us
    all_to_all x1, blocking collectives, on_device(): lax.all_to_all(sent, 'tm', 0, 0, axis_index_groups=spans, tiled=True)  18.7 us
    all_to_all x1, blocking collectives, on_device(): lax.all_to_all(quarters, 'tm', 0, 0, axis_index_groups=spans, tiled=True)  12.5 us
    all_gather x1, blocking collectives, on_device(): packed = lax.all_gather(mine, 'lat', axis=0, tiled=True)  7.26 us
    pallas_call x1, Pallas kernels, on_device(): pl.pallas_call(subwindow_kernel, out_shape=jax.ShapeDtypeStruct((SPAN * K...  2.58 us

profile of v4, /device:TPU:8, one launch (start us, length us, event | category | flops | bytes accessed | tf_op | source)
XLA Modules:
  0.0 66.7 jit_solution(503736817140313293)
XLA Ops:
  1.9 1.0 %shard_map.95 = f32[88,384]{1,0:T(8,128)S(1)} custom-call(f32[32,384]{1,0:T(8,128)} %bitcast.25, f32[48,384]{1,0:T(8,128)} %bitcast.24, s32[8,128]{1,0:T(8,128)} %bitcast.26, f32[8,128]{1,0:T(8,128)} %bitcast.27, f32[8,128]{1,0:T(8,128)} %bitcast.28, s32[1,1]{1,0:T(1,128)S(6)} %copy.10.count), custom_call_target="tpu_custom_call" | custom-call | tf_op jit(solution)/shard_map/pallas_call | solution.py:325
  2.9 0.0 copy-start
  2.9 7.3 %all_gather.3.packed = f32[352,384]{1,0:T(8,128)S(1)} all-gather(f32[88,384]{1,0:T(8,128)S(1)} %shard_map.95), channel_id=1, replica_groups=mesh['tm'=128,'lat'=4] {'lat'}, dimensions={0}, use_global_device_ids=true | all-gather | bytes 675840 | tf_op jit(solution)/shard_map/all_gather | solution.py:349
  10.2 0.0 copy-done
  10.2 2.6 %shard_map.96 = f32[384,128]{1,0:T(8,128)S(1)} custom-call(s32[1,1]{1,0:T(1,128)} %bitcast.15.obs_step, f32[352,384]{1,0:T(8,128)S(1)} %all_gather.3.packed, f32[4,8,384]{2,1,0:T(8,128)S(1)} %bitcast.23), custom_call_target="tpu_custom_call" | custom-call | tf_op jit(solution)/shard_map/pallas_call | solution.py:352
  12.8 18.7 %all_to_all.21 = f32[16,24,128]{2,1,0:T(8,128)S(1)} all-to-all(f32[16,24,128]{2,1,0:T(8,128)S(1)} %bitcast.18), channel_id=1, replica_groups={{0,4,8,12,16,20,24,28,32,36,40,44,48,52,56,60},{64,68,72,76,80,84,88,92..., dimensions={0} | all-to-all | bytes 393216 | tf_op jit(solution)/shard_map/all_to_all | solution.py:359
  31.4 0.1 shard_map.97
  31.5 22.0 %all_to_all.22 = f32[8,9,4,128]{3,2,1,0:T(4,128)S(1)} all-to-all(f32[8,9,4,128]{3,2,1,0:T(4,128)S(1)} %bitcast.20), channel_id=1, replica_groups={{0,64,128,192,256,320,384,448},{4,68,132,196,260,324,388,452},{8,72,136..., dimensions={0} | all-to-all | bytes 294912 | tf_op jit(solution)/shard_map/all_to_all | solution.py:368
  53.4 0.1 shard_map.98
  53.5 12.5 %all_to_all.23 = f32[16,3,4,128]{3,2,1,0:T(4,128)S(1)} all-to-all(f32[16,3,4,128]{3,2,1,0:T(4,128)S(1)} %bitcast.22), channel_id=1, replica_groups={{0,4,8,12,16,20,24,28,32,36,40,44,48,52,56,60},{64,68,72,76,80,84,88,92..., dimensions={0} | all-to-all | bytes 196608 | tf_op jit(solution)/shard_map/all_to_all | solution.py:377
  66.1 0.6 shard_map.99
Async XLA Ops:
  2.9 7.3 %copy-start = (f32[1,4,8,384]{3,2,1,0:T(8,128)S(1)}, f32[1,4,8,384]{3,2,1,0:T(8,128)}, u32[]{:S(2)}) copy-start(f32[1,4,8,384]{3,2,1,0:T(8,128)} %param.9) | copy-start | bytes 147460

commit v5 on v4

--- a/solution.py
+++ b/solution.py
@@ -24,6 +24,7 @@
 MAPS = 6
 MAP_ROWS = MAPS * SHARE
 CHUNK = 512
+PARTS = ROWS * LANE // CHUNK
 
 
 def lon_roll(field, by):
@@ -89,9 +90,9 @@
         copy.wait()
 
 
-def subwindow_kernel(obs_step, packed, rates, out):
+def subwindow_kernel(obs_step, packed, rates, out, picks):
     slab = lax.axis_index("lat")
-    obs_at = jnp.broadcast_to(obs_step[...], (WIN, LON))
+    obs_at = obs_step[0]
 
     def window(base):
         parts = []
@@ -119,42 +120,19 @@
         "forward": (kx - ax, kw + aw, ky - by, ks + bs),
         "backward": (kx + ax, kw - aw, ky + by, ks - bs),
     }
-    state = inc
-    seen = inc
-    for turn in range(STEPS):
-        state = step(state, coef, 1.0)
-        if turn == 0:
-            seen = state
-        else:
-            seen = tuple(jnp.where(obs_at == turn + 1, a, b) for a, b in zip(state, seen, strict=True))
-    end = state
-
-    upper = lax.broadcasted_iota(jnp.int32, (ROWS, LON), 0) < ROWS // 2
-
-    def fold(x):
-        ends = jnp.where(upper, x[2 * ROWS :], x[:ROWS])
-        return jnp.concatenate([x[ROWS : 2 * ROWS], ends], axis=0)
-
-    inc, end, seen = (tuple(fold(x) for x in fields) for fields in (inc, end, seen))
-    coef = {name: tuple(fold(x) for x in coef[name]) for name in ("common", "backward")}
-    table = jnp.concatenate(
-        [seen[f][:, t * LANE : (t + 1) * LANE] for t in range(TILES) for f in range(FIELDS)], axis=0
-    )
-    high = table.shape[0]
-    table_parts = jnp.concatenate(split(jnp.transpose(table)), axis=0)
-
+    high = FIELDS * MID * TILES
     half = jnp.bfloat16
     hi_iota = lax.broadcasted_iota(jnp.int32, (high, CHUNK), 0).astype(half)
-    lo_iota = lax.broadcasted_iota(jnp.int32, (LANE, CHUNK), 0)
-    lo_half = lo_iota.astype(half)
     one, none = jnp.ones((high, CHUNK), half), jnp.zeros((high, CHUNK), half)
-    picks, places = [], []
-    for owner in range(SLABS):
+
+    def wide(x, part):
+        first = part * (CHUNK // LANE)
+        rows = range(first, first + CHUNK // LANE)
+        return jnp.concatenate([x[r : r + 1, :] for r in rows], axis=1)
+
+    def choose(owner):
         base = owner * PACK + 10 * ROWS
         cell = packed[base : base + ROWS, 0:LANE].astype(jnp.int32)
-        value = packed[base : base + ROWS, LANE : 2 * LANE]
-        weight = packed[base : base + ROWS, 2 * LANE : 3 * LANE]
-        low = jnp.bitwise_and(cell, LANE - 1)
         tile_row = jnp.right_shift(cell, 7)
         field_row = jnp.right_shift(tile_row * 21846, 16)
         tile = tile_row - field_row * TILES
@@ -163,30 +141,67 @@
         near = jnp.logical_and(rel >= -(ROWS // 2), rel < ROWS + ROWS // 2)
         place = tile * (FIELDS * MID) + field * MID + jnp.bitwise_and(rel, MID - 1)
         spot = jnp.where(near, place, -1)
-        for pair in range(ROWS // 4):
-            rows = tuple(range(4 * pair, 4 * pair + 4))
-            def wide(x):
-                return jnp.concatenate([x[r : r + 1, :] for r in rows], axis=1)
-
-            here, column = wide(spot), wide(low)
-            pick = jnp.where(hi_iota == here.astype(half), one, none)
-            match = lo_iota == column
-            match_half = lo_half == column.astype(half)
+        for part in range(PARTS):
+            at = (owner * PARTS + part) * CHUNK
+            here = wide(spot, part).astype(half)
+            picks[:, at : at + CHUNK] = jnp.where(hi_iota == here, one, none)
+        return jnp.bitwise_and(cell, LANE - 1)
+
+    lows = []
+    state = inc
+    seen = inc
+    for turn in range(STEPS):
+        state = step(state, coef, 1.0)
+        lows.append(choose(turn))
+        if turn == 0:
+            seen = state
+        else:
+            seen = tuple(jnp.where(obs_at == turn + 1, a, b) for a, b in zip(state, seen, strict=True))
+    end = state
+
+    upper = lax.broadcasted_iota(jnp.int32, (ROWS, LON), 0) < ROWS // 2
+
+    def fold(x):
+        ends = jnp.where(upper, x[2 * ROWS :], x[:ROWS])
+        return jnp.concatenate([x[ROWS : 2 * ROWS], ends], axis=0)
+
+    inc, end, seen = (tuple(fold(x) for x in fields) for fields in (inc, end, seen))
+    coef = {name: tuple(fold(x) for x in coef[name]) for name in ("common", "backward")}
+    table = jnp.concatenate(
+        [seen[f][:, t * LANE : (t + 1) * LANE] for t in range(TILES) for f in range(FIELDS)], axis=0
+    )
+    table_parts = jnp.concatenate(split(jnp.transpose(table)), axis=0)
+
+    lo_iota = lax.broadcasted_iota(jnp.int32, (LANE, CHUNK), 0)
+    lo_half = lo_iota.astype(half)
+    places = []
+    for owner in range(SLABS):
+        base = owner * PACK + 10 * ROWS
+        value = packed[base : base + ROWS, LANE : 2 * LANE]
+        weight = packed[base : base + ROWS, 2 * LANE : 3 * LANE]
+        for part in range(PARTS):
+            at = (owner * PARTS + part) * CHUNK
+            column = wide(lows[owner], part)
             columns = lax.dot_general(
-                table_parts, pick, (((1,), (0,)), ((), ())), preferred_element_type=jnp.float32
+                table_parts,
+                picks[:, at : at + CHUNK],
+                (((1,), (0,)), ((), ())),
+                preferred_element_type=jnp.float32,
             )
             columns = columns[:LANE] + columns[LANE:]
-            sampled = jnp.sum(jnp.where(match, columns, 0.0), axis=0, keepdims=True)
-            depart = wide(weight) * (sampled - wide(value))
+            here = jnp.where(lo_iota == column, columns, 0.0)
+            sampled = jnp.sum(here, axis=0, keepdims=True)
+            depart = wide(weight, part) * (sampled - wide(value, part))
             big = depart.astype(half)
             small = (depart - big.astype(jnp.float32)).astype(half)
-            placed = jnp.concatenate(
-                [jnp.where(match_half, part, none[:LANE]) for part in (big, small)], axis=0
+            match = lo_half == column.astype(half)
+            places.append(
+                jnp.concatenate(
+                    [jnp.where(match, piece, none[:LANE]) for piece in (big, small)], axis=0
+                )
             )
-            picks.append(pick)
-            places.append(placed)
     forcing = lax.dot_general(
-        jnp.concatenate(picks, axis=1),
+        picks[...],
         jnp.concatenate(places, axis=1),
         (((1,), (1,)), ((), ())),
         preferred_element_type=jnp.float32,
@@ -209,7 +224,7 @@
     )
 
     def push(state, turn):
-        scale = jnp.where(obs_at[:MID] == turn, 1.0, 0.0)
+        scale = jnp.where(obs_at == turn, 1.0, 0.0)
         return tuple(a + scale * b for a, b in zip(state, inject, strict=True))
 
     follows = jnp.where(lax.axis_index("tm") < TIMES - 1, 1.0, 0.0)
@@ -352,10 +367,13 @@
     sent = pl.pallas_call(
         subwindow_kernel,
         out_shape=jax.ShapeDtypeStruct((SPAN * KINDS * SHARE, LANE), jnp.float32),
-        in_specs=[vmem] * 3,
+        in_specs=[pl.BlockSpec(memory_space=pltpu.SMEM), vmem, vmem],
         out_specs=vmem,
+        scratch_shapes=[
+            pltpu.VMEM((FIELDS * MID * TILES, SLABS * ROWS * LANE), jnp.bfloat16)
+        ],
         compiler_params=limit,
-    )(obs_step.reshape(1, 1), packed, correlation[0])
+    )(obs_step, packed, correlation[0])
     owned = lax.all_to_all(sent, "tm", 0, 0, axis_index_groups=spans, tiled=True)
     reduced = pl.pallas_call(
         block_kernel,

time: 67 us -> 67 us (level)
  no operation moved by 1% of the time
where the time goes in v5:
time: 67 us; the launch traced here: 66.7 us
  blocking collectives  60.4 us (90%)
  Pallas kernels  4.34 us (6%)
  between operations  1.95 us (3%)
    all_to_all x1, blocking collectives, on_device(): lax.all_to_all(quarters, 'tm', 0, 0, axis_index_groups=strides, tiled=True)  22 us
    all_to_all x1, blocking collectives, on_device(): lax.all_to_all(sent, 'tm', 0, 0, axis_index_groups=spans, tiled=True)  18.6 us
    all_to_all x1, blocking collectives, on_device(): lax.all_to_all(quarters, 'tm', 0, 0, axis_index_groups=spans, tiled=True)  12.5 us
    all_gather x1, blocking collectives, on_device(): packed = lax.all_gather(mine, 'lat', axis=0, tiled=True)  7.26 us
    pallas_call x1, Pallas kernels, on_device(): pl.pallas_call(subwindow_kernel, out_shape=jax.ShapeDtypeStruct((SPAN * K...  2.56 us

profile of v5, /device:TPU:8, one launch (start us, length us, event | category | flops | bytes accessed | tf_op | source)
XLA Modules:
  0.0 66.7 jit_solution(10919443127769755845)
XLA Ops:
  1.9 1.0 %shard_map.95 = f32[88,384]{1,0:T(8,128)S(1)} custom-call(f32[32,384]{1,0:T(8,128)} %bitcast.23, f32[48,384]{1,0:T(8,128)} %bitcast.22, s32[8,128]{1,0:T(8,128)} %bitcast.24, f32[8,128]{1,0:T(8,128)} %bitcast.25, f32[8,128]{1,0:T(8,128)} %bitcast.26, s32[1,1]{1,0:T(1,128)S(6)} %copy.10.count), custom_call_target="tpu_custom_call" | custom-call | tf_op jit(solution)/shard_map/pallas_call | solution.py:340
  2.9 0.0 copy-start
  2.9 7.3 %all_gather.3.packed = f32[352,384]{1,0:T(8,128)S(1)} all-gather(f32[88,384]{1,0:T(8,128)S(1)} %shard_map.95), channel_id=1, replica_groups=mesh['tm'=128,'lat'=4] {'lat'}, dimensions={0}, use_global_device_ids=true | all-gather | bytes 675840 | tf_op jit(solution)/shard_map/all_gather | solution.py:364
  10.2 0.0 copy-done
  10.2 2.6 %shard_map.96 = f32[384,128]{1,0:T(8,128)S(1)} custom-call(s32[1]{0:T(128)S(6)} %copy.11.obs_step, f32[352,384]{1,0:T(8,128)S(1)} %all_gather.3.packed, f32[4,8,384]{2,1,0:T(8,128)S(1)} %bitcast.21), custom_call_target="tpu_custom_call" | custom-call | tf_op jit(solution)/shard_map/pallas_call | solution.py:367
  12.7 18.6 %all_to_all.21 = f32[16,24,128]{2,1,0:T(8,128)S(1)} all-to-all(f32[16,24,128]{2,1,0:T(8,128)S(1)} %bitcast.16), channel_id=1, replica_groups={{0,4,8,12,16,20,24,28,32,36,40,44,48,52,56,60},{64,68,72,76,80,84,88,92..., dimensions={0} | all-to-all | bytes 393216 | tf_op jit(solution)/shard_map/all_to_all | solution.py:377
  31.4 0.1 shard_map.97
  31.5 22.0 %all_to_all.22 = f32[8,9,4,128]{3,2,1,0:T(4,128)S(1)} all-to-all(f32[8,9,4,128]{3,2,1,0:T(4,128)S(1)} %bitcast.18), channel_id=1, replica_groups={{0,64,128,192,256,320,384,448},{4,68,132,196,260,324,388,452},{8,72,136..., dimensions={0} | all-to-all | bytes 294912 | tf_op jit(solution)/shard_map/all_to_all | solution.py:386
  53.4 0.1 shard_map.98
  53.5 12.5 %all_to_all.23 = f32[16,3,4,128]{3,2,1,0:T(4,128)S(1)} all-to-all(f32[16,3,4,128]{3,2,1,0:T(4,128)S(1)} %bitcast.20), channel_id=1, replica_groups={{0,4,8,12,16,20,24,28,32,36,40,44,48,52,56,60},{64,68,72,76,80,84,88,92..., dimensions={0} | all-to-all | bytes 196608 | tf_op jit(solution)/shard_map/all_to_all | solution.py:395
  66.1 0.6 shard_map.99
Async XLA Ops:
  2.9 7.3 %copy-start = (f32[1,4,8,384]{3,2,1,0:T(8,128)S(1)}, f32[1,4,8,384]{3,2,1,0:T(8,128)}, u32[]{:S(2)}) copy-start(f32[1,4,8,384]{3,2,1,0:T(8,128)} %param.9) | copy-start | bytes 147460

commit v6 on v4

--- a/solution.py
+++ b/solution.py
@@ -356,7 +356,9 @@
         out_specs=vmem,
         compiler_params=limit,
     )(obs_step.reshape(1, 1), packed, correlation[0])
-    owned = lax.all_to_all(sent, "tm", 0, 0, axis_index_groups=spans, tiled=True)
+    owned = lax.all_to_all(
+        sent.reshape(SPAN, -1, 2, LANE), "tm", 0, 0, axis_index_groups=spans, tiled=True
+    ).reshape(sent.shape)
     reduced = pl.pallas_call(
         block_kernel,
         out_shape=jax.ShapeDtypeStruct((BLOCKS * MAP_ROWS, LANE), jnp.float32),

time: 67 us -> 67 us (level)
  no operation moved by 1% of the time
where the time goes in v6:
time: 67 us; the launch traced here: 66.7 us
  blocking collectives  60.4 us (90%)
  Pallas kernels  4.36 us (7%)
  between operations  1.95 us (3%)
    all_to_all x1, blocking collectives, on_device(): lax.all_to_all(quarters, 'tm', 0, 0, axis_index_groups=strides, tiled=True)  22 us
    all_to_all x1, blocking collectives, on_device(): lax.all_to_all(sent.reshape(SPAN, -1, 2, LANE), 'tm', 0, 0, axis_index_gr...  18.7 us
    all_to_all x1, blocking collectives, on_device(): lax.all_to_all(quarters, 'tm', 0, 0, axis_index_groups=spans, tiled=True)  12.5 us
    all_gather x1, blocking collectives, on_device(): packed = lax.all_gather(mine, 'lat', axis=0, tiled=True)  7.26 us
    pallas_call x1, Pallas kernels, on_device(): pl.pallas_call(subwindow_kernel, out_shape=jax.ShapeDtypeStruct((SPAN * K...  2.58 us

profile of v6, /device:TPU:8, one launch (start us, length us, event | category | flops | bytes accessed | tf_op | source)
XLA Modules:
  0.0 66.7 jit_solution(503736817140313293)
XLA Ops:
  1.9 1.0 %shard_map.95 = f32[88,384]{1,0:T(8,128)S(1)} custom-call(f32[32,384]{1,0:T(8,128)} %bitcast.25, f32[48,384]{1,0:T(8,128)} %bitcast.24, s32[8,128]{1,0:T(8,128)} %bitcast.26, f32[8,128]{1,0:T(8,128)} %bitcast.27, f32[8,128]{1,0:T(8,128)} %bitcast.28, s32[1,1]{1,0:T(1,128)S(6)} %copy.10.count), custom_call_target="tpu_custom_call" | custom-call | tf_op jit(solution)/shard_map/pallas_call | solution.py:325
  2.9 0.0 copy-start
  2.9 7.3 %all_gather.3.packed = f32[352,384]{1,0:T(8,128)S(1)} all-gather(f32[88,384]{1,0:T(8,128)S(1)} %shard_map.95), channel_id=1, replica_groups=mesh['tm'=128,'lat'=4] {'lat'}, dimensions={0}, use_global_device_ids=true | all-gather | bytes 675840 | tf_op jit(solution)/shard_map/all_gather | solution.py:349
  10.2 0.0 copy-done
  10.2 2.6 %shard_map.96 = f32[384,128]{1,0:T(8,128)S(1)} custom-call(s32[1,1]{1,0:T(1,128)} %bitcast.15.obs_step, f32[352,384]{1,0:T(8,128)S(1)} %all_gather.3.packed, f32[4,8,384]{2,1,0:T(8,128)S(1)} %bitcast.23), custom_call_target="tpu_custom_call" | custom-call | tf_op jit(solution)/shard_map/pallas_call | solution.py:352
  12.8 18.7 %all_to_all.15 = f32[16,12,2,128]{3,2,1,0:T(2,128)S(1)} all-to-all(f32[16,12,2,128]{3,2,1,0:T(2,128)S(1)} %bitcast.18), channel_id=1, replica_groups={{0,4,8,12,16,20,24,28,32,36,40,44,48,52,56,60},{64,68,72,76,80,84,88,92..., dimensions={0} | all-to-all | bytes 393216 | tf_op jit(solution)/shard_map/all_to_all | solution.py:359
  31.4 0.1 shard_map.97
  31.5 22.0 %all_to_all.16 = f32[8,9,4,128]{3,2,1,0:T(4,128)S(1)} all-to-all(f32[8,9,4,128]{3,2,1,0:T(4,128)S(1)} %bitcast.20), channel_id=1, replica_groups={{0,64,128,192,256,320,384,448},{4,68,132,196,260,324,388,452},{8,72,136..., dimensions={0} | all-to-all | bytes 294912 | tf_op jit(solution)/shard_map/all_to_all | solution.py:370
  53.4 0.1 shard_map.98
  53.5 12.5 %all_to_all.17 = f32[16,3,4,128]{3,2,1,0:T(4,128)S(1)} all-to-all(f32[16,3,4,128]{3,2,1,0:T(4,128)S(1)} %bitcast.22), channel_id=1, replica_groups={{0,4,8,12,16,20,24,28,32,36,40,44,48,52,56,60},{64,68,72,76,80,84,88,92..., dimensions={0} | all-to-all | bytes 196608 | tf_op jit(solution)/shard_map/all_to_all | solution.py:379
  66.1 0.6 shard_map.99
Async XLA Ops:
  2.9 7.3 %copy-start = (f32[1,4,8,384]{3,2,1,0:T(8,128)S(1)}, f32[1,4,8,384]{3,2,1,0:T(8,128)}, u32[]{:S(2)}) copy-start(f32[1,4,8,384]{3,2,1,0:T(8,128)} %param.9) | copy-start | bytes 147460

commit v7 on v4

--- a/solution.py
+++ b/solution.py
@@ -307,13 +307,19 @@
             out[first : first + SHARE, :] = value
 
 
-def unpack_kernel(parts, gradient, direction):
+def unpack_kernel(parts, gradient, direction, held, sems):
+    copies = []
     for e, out in enumerate((gradient, direction)):
         for f in range(FIELDS):
             half, odd = divmod(f, 2)
             for t in range(TILES):
                 first = half * ROWS * 2 * SHARE + e * SHARE + odd * TILES + t
-                out[f, :, t * LANE : (t + 1) * LANE] = parts[pl.ds(first, ROWS, stride=2 * SHARE), :]
+                tile = parts[pl.ds(first, ROWS, stride=2 * SHARE), :]
+                held[e, f, :, t * LANE : (t + 1) * LANE] = tile
+        copies.append(pltpu.make_async_copy(held.at[e], out, sems.at[e]))
+        copies[-1].start()
+    for copy in copies:
+        copy.wait()
 
 
 def on_device(
@@ -380,7 +386,11 @@
         unpack_kernel,
         out_shape=(shape, shape),
         in_specs=[vmem],
-        out_specs=(vmem, vmem),
+        out_specs=(far, far),
+        scratch_shapes=[
+            pltpu.VMEM((2, FIELDS, ROWS, LON), jnp.float32),
+            pltpu.SemaphoreType.DMA((2,)),
+        ],
         compiler_params=limit,
     )(returned.reshape(SPAN * 2 * SHARE, LANE))
     return gradient[None], direction[None]

time: 67 us -> 67.1 us (level)
  no operation moved by 1% of the time
where the time goes in v7:
time: 67.1 us; the launch traced here: 66.7 us
  blocking collectives  60.4 us (90%)
  Pallas kernels  4.37 us (7%)
  between operations  1.95 us (3%)
    all_to_all x1, blocking collectives, on_device(): lax.all_to_all(quarters, 'tm', 0, 0, axis_index_groups=strides, tiled=True)  22 us
    all_to_all x1, blocking collectives, on_device(): lax.all_to_all(sent, 'tm', 0, 0, axis_index_groups=spans, tiled=True)  18.7 us
    all_to_all x1, blocking collectives, on_device(): lax.all_to_all(quarters, 'tm', 0, 0, axis_index_groups=spans, tiled=True)  12.5 us
    all_gather x1, blocking collectives, on_device(): packed = lax.all_gather(mine, 'lat', axis=0, tiled=True)  7.26 us
    pallas_call x1, Pallas kernels, on_device(): pl.pallas_call(subwindow_kernel, out_shape=jax.ShapeDtypeStruct((SPAN * K...  2.58 us

profile of v7, /device:TPU:8, one launch (start us, length us, event | category | flops | bytes accessed | tf_op | source)
XLA Modules:
  0.0 66.7 jit_solution(10575003300156456851)
XLA Ops:
  1.9 1.0 %shard_map.95 = f32[88,384]{1,0:T(8,128)S(1)} custom-call(f32[32,384]{1,0:T(8,128)} %bitcast.25, f32[48,384]{1,0:T(8,128)} %bitcast.24, s32[8,128]{1,0:T(8,128)} %bitcast.26, f32[8,128]{1,0:T(8,128)} %bitcast.27, f32[8,128]{1,0:T(8,128)} %bitcast.28, s32[1,1]{1,0:T(1,128)S(6)} %copy.10.count), custom_call_target="tpu_custom_call" | custom-call | tf_op jit(solution)/shard_map/pallas_call | solution.py:331
  2.9 0.0 copy-start
  2.9 7.3 %all_gather.3.packed = f32[352,384]{1,0:T(8,128)S(1)} all-gather(f32[88,384]{1,0:T(8,128)S(1)} %shard_map.95), channel_id=1, replica_groups=mesh['tm'=128,'lat'=4] {'lat'}, dimensions={0}, use_global_device_ids=true | all-gather | bytes 675840 | tf_op jit(solution)/shard_map/all_gather | solution.py:355
  10.2 0.0 copy-done
  10.2 2.6 %shard_map.96 = f32[384,128]{1,0:T(8,128)S(1)} custom-call(s32[1,1]{1,0:T(1,128)} %bitcast.15.obs_step, f32[352,384]{1,0:T(8,128)S(1)} %all_gather.3.packed, f32[4,8,384]{2,1,0:T(8,128)S(1)} %bitcast.23), custom_call_target="tpu_custom_call" | custom-call | tf_op jit(solution)/shard_map/pallas_call | solution.py:358
  12.8 18.7 %all_to_all.21 = f32[16,24,128]{2,1,0:T(8,128)S(1)} all-to-all(f32[16,24,128]{2,1,0:T(8,128)S(1)} %bitcast.18), channel_id=1, replica_groups={{0,4,8,12,16,20,24,28,32,36,40,44,48,52,56,60},{64,68,72,76,80,84,88,92..., dimensions={0} | all-to-all | bytes 393216 | tf_op jit(solution)/shard_map/all_to_all | solution.py:365
  31.4 0.1 shard_map.97
  31.5 22.0 %all_to_all.22 = f32[8,9,4,128]{3,2,1,0:T(4,128)S(1)} all-to-all(f32[8,9,4,128]{3,2,1,0:T(4,128)S(1)} %bitcast.20), channel_id=1, replica_groups={{0,64,128,192,256,320,384,448},{4,68,132,196,260,324,388,452},{8,72,136..., dimensions={0} | all-to-all | bytes 294912 | tf_op jit(solution)/shard_map/all_to_all | solution.py:374
  53.4 0.1 shard_map.98
  53.5 12.5 %all_to_all.23 = f32[16,3,4,128]{3,2,1,0:T(4,128)S(1)} all-to-all(f32[16,3,4,128]{3,2,1,0:T(4,128)S(1)} %bitcast.22), channel_id=1, replica_groups={{0,4,8,12,16,20,24,28,32,36,40,44,48,52,56,60},{64,68,72,76,80,84,88,92..., dimensions={0} | all-to-all | bytes 196608 | tf_op jit(solution)/shard_map/all_to_all | solution.py:383
  66.1 0.7 shard_map.99
Async XLA Ops:
  2.9 7.3 %copy-start = (f32[1,4,8,384]{3,2,1,0:T(8,128)S(1)}, f32[1,4,8,384]{3,2,1,0:T(8,128)}, u32[]{:S(2)}) copy-start(f32[1,4,8,384]{3,2,1,0:T(8,128)} %param.9) | copy-start | bytes 147460
